TPU v7x, 32 devices: a whole 2x2x4 slice. The times are simulated.
32 devices in a mesh: groups: 2 (over y), depth: 4 (over z), rays: 4 (over x, core).
Axes of the slice: x: 2, y: 2, z: 4, core: 2. Of those that a mesh axis runs over, the one named last changes fastest.
Arguments:
- brick_features: bfloat16 [16, 8, 4, 16384], P(None, ('groups', 'depth'), 'rays'), parts along dimension 1, may hold values from -6 to 6
- entry_cells: int32 [8, 4, 1024], P(('groups', 'depth'), 'rays'), parts along dimension 0, may hold values from 0 to 16368
- sample_counts: int32 [8, 4, 1024], P(('groups', 'depth'), 'rays'), parts along dimension 0, may hold values from 1 to 16, as said below
- brick_rank: int32 [8, 4], P(('groups', 'rays')), parts along dimension 0, may hold values from 0 to 3, each once within a row
- input_layer_weight: bfloat16 [16, 128], replicated, may hold values from -1.5 to 1.5
- second_weight: bfloat16 [128, 33], replicated, may hold values from -0.5 to 0.5
- conv_in: bfloat16 [9, 32, 128], replicated, may hold values from -0.375 to 0.375
- conv_mid: bfloat16 [9, 128, 128], replicated, may hold values from -0.1875 to 0.1875
- conv_out: bfloat16 [9, 128, 128], replicated, may hold values from -0.1875 to 0.1875
Outputs:
- frame: bfloat16 [128, 64, 128], P(('groups', 'depth'), 'rays'), parts along dimension 0
There are 2 independent parts, one for each index of `groups`. A program takes and returns all parts, laid end to end along the dimension named above; an argument that names none is the same for every part. Nothing has to cross between parts.
Inputs may be any that keep to these rules, and one draw needn't show every extreme that they name: `sample_counts`: each brick and strip has a level of at most 16; its rays take 1 to that level samples; some brick and strip reaches 16. `brick_rank`: each row is a permutation of the bricks.
All inputs are finite; a program needn't handle non-finite values.
Results may differ from a plain program's by a relative error of at most 0.015.
Values may be sent and summed in bfloat16 or wider, within the bound.
A program may use at most 64 MiB of HBM per device.

v0:
```python
import math
import jax
import jax.numpy as jnp
from jax import lax
from jax.sharding import PartitionSpec as P

SAMPLES = 16
ROWS_OWN = 16
COLS_DEV = 16


def padded_2(x, sides, width):
    for axis, dim in sides:
        size, length = (lax.axis_size(axis), x.shape[dim])
        up = [(i, (i + 1) % size) for i in range(size - 1)]
        down = [(j, i) for i, j in up]
        last = lax.slice_in_dim(x, length - width, length, axis=dim)
        first = lax.slice_in_dim(x, 0, width, axis=dim)
        before = lax.ppermute(last, axis, up)
        after = lax.ppermute(first, axis, down)
        x = jnp.concatenate([before, x, after], axis=dim)
    return x


def blend_sample_values(field, counts, bricks):
    step_len = 8.0 / (SAMPLES * bricks)
    slot_ids = jnp.arange(SAMPLES, dtype=jnp.int32)
    valid = (slot_ids[:, None] < counts[None, :]).astype(jnp.float32)
    optical = step_len * jax.nn.softplus(field[0]) * valid
    earlier = (slot_ids[:, None] > slot_ids[None, :]).astype(jnp.float32)
    before = jnp.dot(earlier, optical, precision=lax.Precision.HIGHEST)
    weights = jnp.exp(-before) * (1.0 - jnp.exp(-optical))
    colour = jnp.sum(weights[None] * field[1:], axis=1)
    return (colour, jnp.sum(optical, axis=0))


def convolve_valid(padded, weights):
    height = padded.shape[0] - 2
    width = padded.shape[1] - 2
    total = jnp.zeros((height * width, weights.shape[2]), jnp.float32)
    for tap in range(9):
        row_offset_shift, shift_col = divmod(tap, 3)
        window = padded[
            row_offset_shift : row_offset_shift + height, shift_col : shift_col + width
        ].reshape(height * width, -1)
        total = total + jnp.dot(window, weights[tap], preferred_element_type=jnp.float32)
    return total.reshape(height, width, weights.shape[2])


def border_padding(source):
    return padded_2(source, (("depth", 0), ("rays", 1)), 1)


def shards(
    brick_features,
    entry_cells,
    sample_counts,
    brick_rank,
    input_layer_weight,
    second_weight,
    conv_in,
    conv_mid,
    conv_out,
):
    bricks = lax.axis_size("depth")
    feat_count = brick_features.shape[0]
    cell_count = brick_features.shape[3]
    windows = cell_count // SAMPLES
    span = SAMPLES * feat_count
    table = (
        brick_features.reshape(feat_count, windows, SAMPLES)
        .transpose(1, 2, 0)
        .reshape(windows, span)
    )
    entries = entry_cells.reshape(-1)
    counts = sample_counts.reshape(-1)
    ranks = brick_rank.reshape(-1)
    total_rays = entries.shape[0]
    block = math.gcd(total_rays, 512)
    shift_bits = (SAMPLES - 1).bit_length()

    def march_block(operands):
        block_entries, block_counts = operands
        window_ids = block_entries // SAMPLES
        offset = block_entries - window_ids * SAMPLES
        following = jnp.minimum(window_ids + 1, windows - 1)
        paired = jnp.concatenate(
            [jnp.take(table, window_ids, axis=0), jnp.take(table, following, axis=0)], axis=1
        )
        for level in range(shift_bits):
            moved_by = (1 << level) * feat_count
            moved = jnp.concatenate(
                [paired[:, moved_by:], jnp.zeros((block, moved_by), paired.dtype)], axis=1
            )
            taken = (offset >> level & 1)[:, None] == 1
            paired = jnp.where(taken, moved, paired)
        probed_values = paired[:, :span].reshape(block, SAMPLES, feat_count)
        before_activation = jnp.einsum(
            "fh,isf->hsi", input_layer_weight, probed_values, preferred_element_type=jnp.float32
        )
        hidden = (
            jnp.maximum(before_activation, 0.0).astype(jnp.bfloat16).reshape(-1, SAMPLES * block)
        )
        field = jnp.einsum("ho,hn->on", second_weight, hidden, preferred_element_type=jnp.float32)
        return blend_sample_values(field.reshape(-1, SAMPLES, block), block_counts, bricks)

    colour_blocks, depth_blocks = lax.map(
        march_block, (entries.reshape(-1, block), counts.reshape(-1, block))
    )
    colour = jnp.transpose(colour_blocks, (1, 0, 2)).reshape(colour_blocks.shape[1], total_rays)
    depth_sum = depth_blocks.reshape(1, total_rays)
    all_depth = lax.all_gather(depth_sum, "depth", axis=0, tiled=True)
    my_rank = ranks[lax.axis_index("depth")]
    ahead = (ranks < my_rank).astype(jnp.float32)[None, :]
    front = jnp.dot(ahead, all_depth, precision=lax.Precision.HIGHEST)
    image = lax.psum_scatter(
        (colour * jnp.exp(-front)).astype(jnp.bfloat16), "depth", scatter_dimension=1, tiled=True
    ).astype(jnp.float32)
    image = image.reshape(-1, ROWS_OWN, COLS_DEV).transpose(1, 2, 0).astype(jnp.bfloat16)
    first = jnp.maximum(convolve_valid(border_padding(image), conv_in), 0.0).astype(jnp.bfloat16)
    second = jnp.maximum(convolve_valid(border_padding(first), conv_mid), 0.0).astype(jnp.bfloat16)
    frame = convolve_valid(border_padding(second), conv_out).astype(jnp.bfloat16)
    return frame


def solution(mesh):
    placed = (
        P(None, ("groups", "depth"), "rays", None),
        P(("groups", "depth"), "rays", None),
        P(("groups", "depth"), "rays", None),
        P(("groups", "rays"), None),
        P(),
        P(),
        P(),
        P(),
        P(),
    )
    return jax.shard_map(
        shards,
        mesh=mesh,
        in_specs=placed,
        out_specs=P(("groups", "depth"), "rays", None),
        check_vma=False,
    )
```

profile of v0, /device:TPU:1, one launch (start us, length us, event | category | flops | bytes accessed | tf_op | source)
XLA Modules:
  0.0 133.9 jit_solution(3947614905401499600)
XLA Ops:
  9.6 5.4 %reshape.274 = bf16[16,1024,16]{2,1,0:T(8,128)(2,1)} reshape(bf16[16,1,1,16384]{3,0,2,1:T(8,128)(2,1)} %param.13) | data formatting | bytes 1048576 | tf_op jit(solution)/shard_map/reshape | solution.py:71
  15.1 3.7 %copy.18 = bf16[1024,16,16]{0,2,1:T(8,128)(2,1)S(1)} copy(bf16[1024,16,16]{1,0,2:T(8,128)(2,1)} %bitcast.218) | data formatting | bytes 1048576 | tf_op jit(solution)/shard_map/transpose | solution.py:72
  19.0 19.6 %while.14 = (s32[]{:T(128)}, f32[2,32,512]{2,1,0:T(8,128)S(1)}, f32[2,512]{1,0:T(2,128)S(1)}, s32[2,512]{1,0:T(2,128)S(1)}, s32[2,512]{1,0:T(2,128)S(1)}, /*inde...) while((s32[]{:T(128)}, f32[2,32,512]{2,1,0:T(8,128)S(1)}, ...), condition=%wide.region_3.5_spmd, body=%wide.region_0.4_spmd.sunk | while | flops 110472448 | bytes 23171440 | solution.py:107
  19.1 2.0 %gather_fusion.1 = bf16[512,256]{1,0:T(8,128)(2,1)S(1)} fusion(bf16[1024,256]{1,0:T(8,128)(2,1)S(1)} %get-tuple-element.298, s32[1024]{0:T(1024)S(1)} %pad_clamp_fusion.5), kind=kCustom, calls=%fused_computation.clone.clone.1 | custom fusion | bytes 526336 | tf_op jit(solution)/shard_map/while/body/eval_jaxpr/jit(_take)/gather | solution.py:88
  21.2 2.0 %gather_fusion = bf16[512,256]{1,0:T(8,128)(2,1)S(1)} fusion(bf16[1024,256]{1,0:T(8,128)(2,1)S(1)} %get-tuple-element.298, s32[1024]{0:T(1024)S(1)} %pad_clamp_fusion.4), kind=kCustom, calls=%fused_computation.1.clone.clone.1 | custom fusion | bytes 526336 | tf_op jit(solution)/shard_map/while/body/eval_jaxpr/jit(_take)/gather | solution.py:88
  26.1 1.3 convolution_bitcast_fusion.2
  28.9 2.0 %gather_fusion.1 = bf16[512,256]{1,0:T(8,128)(2,1)S(1)} fusion(bf16[1024,256]{1,0:T(8,128)(2,1)S(1)} %get-tuple-element.298, s32[1024]{0:T(1024)S(1)} %pad_clamp_fusion.5), kind=kCustom, calls=%fused_computation.clone.clone.1 | custom fusion | bytes 526336 | tf_op jit(solution)/shard_map/while/body/eval_jaxpr/jit(_take)/gather | solution.py:88
  31.0 2.0 %gather_fusion = bf16[512,256]{1,0:T(8,128)(2,1)S(1)} fusion(bf16[1024,256]{1,0:T(8,128)(2,1)S(1)} %get-tuple-element.298, s32[1024]{0:T(1024)S(1)} %pad_clamp_fusion.4), kind=kCustom, calls=%fused_computation.1.clone.clone.1 | custom fusion | bytes 526336 | tf_op jit(solution)/shard_map/while/body/eval_jaxpr/jit(_take)/gather | solution.py:88
  38.6 11.3 %all-gather = f32[4,1,1024]{2,1,0:T(1,128)S(1)} all-gather(f32[1,1,1024]{2,1,0:T(1,128)S(1)} %reshape.322), channel_id=1, replica_groups=mesh['groups'=2,'depth'=4,'rays'=4] {'depth'}, dimensions={0}, use_global_device_ids=true | all-gather | bytes 20480 | tf_op jit(solution)/shard_map/all_gather | solution.py:112
  52.0 20.8 %reduce-scatter.2.cloned.1.call-done = bf16[32,256]{1,0:T(8,128)(2,1)} async-done(((bf16[32,1024]{1,0:T(8,128)(2,1)}), bf16[32,256]{1,0:T(8,128)(2,1)}) %reduce-scatter.2.cloned.1.call-update) | async-done | bytes 16400 | tf_op jit(solution)/shard_map/reduce_scatter | solution.py:116
  76.2 3.0 %collective-permute-done.1 = bf16[1,16,32]{2,1,0:T(8,128)(2,1)S(1)} collective-permute-done((bf16[1,16,32]{2,1,0:T(8,128)(2,1)S(1)}, bf16[1,16,32]{2,1,0:T(8,128)(2,1)S(1)}, u32[]{:S(2)}, u32[]{:S(2)}) %collective-permute-start.1) | collective-permute-done | bytes 1056 | tf_op jit(solution)/shard_map/ppermute | solution.py:20
  79.3 7.1 %collective-permute-start.2 = (bf16[18,1,32]{2,1,0:T(2,128)(2,1)S(1)}, bf16[18,1,32]{2,1,0:T(2,128)(2,1)S(1)}, u32[]{:S(2)}, u32[]{:S(2)}) collective-permute-start(bf16[18,1,32]{2,1,0:T(2,128)(2,1)S(1)} %get-tuple-element.183), channel_id=1, source_target_pairs={{0,1},{1,2},{2,3},{4,5},{5,6},{6,7},{8,9},{9,10},{10,11},{12,13},{... | collective-permute-start | bytes 3464 | tf_op jit(solution)/shard_map/ppermute | solution.py:19
  86.4 1.9 %collective-permute-start.3 = (bf16[18,1,32]{2,1,0:T(2,128)(2,1)S(1)}, bf16[18,1,32]{2,1,0:T(2,128)(2,1)S(1)}, u32[]{:S(2)}, u32[]{:S(2)}) collective-permute-start(bf16[18,1,32]{2,1,0:T(2,128)(2,1)S(1)} %get-tuple-element.184), channel_id=1, source_target_pairs={{1,0},{2,1},{3,2},{5,4},{6,5},{7,6},{9,8},{10,9},{11,10},{13,12},{... | collective-permute-start | bytes 3464 | tf_op jit(solution)/shard_map/ppermute | solution.py:20
  88.5 2.9 %collective-permute-done.3 = bf16[18,1,32]{2,1,0:T(2,128)(2,1)S(1)} collective-permute-done((bf16[18,1,32]{2,1,0:T(2,128)(2,1)S(1)}, bf16[18,1,32]{2,1,0:T(2,128)(2,1)S(1)}, u32[]{:S(2)}, u32[]{:S(2)}) %collective-permute-start.3) | collective-permute-done | bytes 1184 | tf_op jit(solution)/shard_map/ppermute | solution.py:20
  92.7 3.4 %collective-permute-start.4 = (bf16[1,16,128]{2,1,0:T(8,128)(2,1)S(1)}, bf16[1,16,128]{2,1,0:T(8,128)(2,1)S(1)}, u32[]{:S(2)}, u32[]{:S(2)}) collective-permute-start(bf16[1,16,128]{2,1,0:T(8,128)(2,1)S(1)} %get-tuple-element.191), channel_id=1, source_target_pairs={{0,4},{4,8},{8,12},{1,5},{5,9},{9,13},{2,6},{6,10},{10,14},{3,7},{... | collective-permute-start | bytes 12296 | tf_op jit(solution)/shard_map/ppermute | solution.py:19
  97.4 3.0 %collective-permute-done.5 = bf16[1,16,128]{2,1,0:T(8,128)(2,1)S(1)} collective-permute-done((bf16[1,16,128]{2,1,0:T(8,128)(2,1)S(1)}, bf16[1,16,128]{2,1,0:T(8,128)(2,1)S(1)}, u32[]{:S(2)}, u32[]{:S(2)}) %collective-permute-start.5) | collective-permute-done | bytes 4128 | tf_op jit(solution)/shard_map/ppermute | solution.py:20
  100.4 3.4 %collective-permute-start.6 = (bf16[18,1,128]{2,1,0:T(2,128)(2,1)S(1)}, bf16[18,1,128]{2,1,0:T(2,128)(2,1)S(1)}, u32[]{:S(2)}, u32[]{:S(2)}) collective-permute-start(bf16[18,1,128]{2,1,0:T(2,128)(2,1)S(1)} %get-tuple-element.179), channel_id=1, source_target_pairs={{0,1},{1,2},{2,3},{4,5},{5,6},{6,7},{8,9},{9,10},{10,11},{12,13},{... | collective-permute-start | bytes 13832 | tf_op jit(solution)/shard_map/ppermute | solution.py:19
  103.8 1.9 %collective-permute-start.7 = (bf16[18,1,128]{2,1,0:T(2,128)(2,1)S(1)}, bf16[18,1,128]{2,1,0:T(2,128)(2,1)S(1)}, u32[]{:S(2)}, u32[]{:S(2)}) collective-permute-start(bf16[18,1,128]{2,1,0:T(2,128)(2,1)S(1)} %get-tuple-element.180), channel_id=1, source_target_pairs={{1,0},{2,1},{3,2},{5,4},{6,5},{7,6},{9,8},{10,9},{11,10},{13,12},{... | collective-permute-start | bytes 13832 | tf_op jit(solution)/shard_map/ppermute | solution.py:20
  106.0 2.9 %collective-permute-done.7 = bf16[18,1,128]{2,1,0:T(2,128)(2,1)S(1)} collective-permute-done((bf16[18,1,128]{2,1,0:T(2,128)(2,1)S(1)}, bf16[18,1,128]{2,1,0:T(2,128)(2,1)S(1)}, u32[]{:S(2)}, u32[]{:S(2)}) %collective-permute-start.7) | collective-permute-done | bytes 4640 | tf_op jit(solution)/shard_map/ppermute | solution.py:20
  110.2 2.1 %collective-permute-start.8 = (bf16[1,16,128]{2,1,0:T(8,128)(2,1)S(1)}, bf16[1,16,128]{2,1,0:T(8,128)(2,1)S(1)}, u32[]{:S(2)}, u32[]{:S(2)}) collective-permute-start(bf16[1,16,128]{2,1,0:T(8,128)(2,1)S(1)} %get-tuple-element.187), channel_id=1, source_target_pairs={{0,4},{4,8},{8,12},{1,5},{5,9},{9,13},{2,6},{6,10},{10,14},{3,7},{... | collective-permute-start | bytes 12296 | tf_op jit(solution)/shard_map/ppermute | solution.py:19
  113.6 3.0 %collective-permute-done.9 = bf16[1,16,128]{2,1,0:T(8,128)(2,1)S(1)} collective-permute-done((bf16[1,16,128]{2,1,0:T(8,128)(2,1)S(1)}, bf16[1,16,128]{2,1,0:T(8,128)(2,1)S(1)}, u32[]{:S(2)}, u32[]{:S(2)}) %collective-permute-start.9) | collective-permute-done | bytes 4128 | tf_op jit(solution)/shard_map/ppermute | solution.py:20
  116.7 3.4 %collective-permute-start.10 = (bf16[18,1,128]{2,1,0:T(2,128)(2,1)S(1)}, bf16[18,1,128]{2,1,0:T(2,128)(2,1)S(1)}, u32[]{:S(2)}, u32[]{:S(2)}) collective-permute-start(bf16[18,1,128]{2,1,0:T(2,128)(2,1)S(1)} %get-tuple-element.175), channel_id=1, source_target_pairs={{0,1},{1,2},{2,3},{4,5},{5,6},{6,7},{8,9},{9,10},{10,11},{12,13},{... | collective-permute-start | bytes 13832 | tf_op jit(solution)/shard_map/ppermute | solution.py:19
  120.1 1.9 %collective-permute-start.11 = (bf16[18,1,128]{2,1,0:T(2,128)(2,1)S(1)}, bf16[18,1,128]{2,1,0:T(2,128)(2,1)S(1)}, u32[]{:S(2)}, u32[]{:S(2)}) collective-permute-start(bf16[18,1,128]{2,1,0:T(2,128)(2,1)S(1)} %get-tuple-element.176), channel_id=1, source_target_pairs={{1,0},{2,1},{3,2},{5,4},{6,5},{7,6},{9,8},{10,9},{11,10},{13,12},{... | collective-permute-start | bytes 13832 | tf_op jit(solution)/shard_map/ppermute | solution.py:20
  122.2 2.9 %collective-permute-done.11 = bf16[18,1,128]{2,1,0:T(2,128)(2,1)S(1)} collective-permute-done((bf16[18,1,128]{2,1,0:T(2,128)(2,1)S(1)}, bf16[18,1,128]{2,1,0:T(2,128)(2,1)S(1)}, u32[]{:S(2)}, u32[]{:S(2)}) %collective-permute-start.11) | collective-permute-done | bytes 4640 | tf_op jit(solution)/shard_map/ppermute | solution.py:20
  (140 shorter events, 26.4 us)
Async XLA Ops:
  6.5 66.3 %reduce-scatter.2.cloned.1.call-start = ((), (), s32[]{:S(2)}) async-start(), calls=%async_computation.1 | async-start | bytes 81920 | tf_op jit(solution)/shard_map/reduce_scatter | solution.py:116
  15.1 3.9 %copy-start.2 = (bf16[128,33]{0,1:T(8,128)(2,1)S(1)}, bf16[128,33]{0,1:T(8,128)(2,1)}, u32[]{:S(2)}) copy-start(bf16[128,33]{0,1:T(8,128)(2,1)} %param.18) | copy-start | bytes 25348
  15.1 3.9 %copy-start.3 = (bf16[16,128]{1,0:T(8,128)(2,1)S(1)}, bf16[16,128]{1,0:T(8,128)(2,1)}, u32[]{:S(2)}) copy-start(bf16[16,128]{1,0:T(8,128)(2,1)} %param.17) | copy-start | bytes 12292
  19.0 30.9 %copy-start.5 = (s32[1,4]{1,0:T(1,128)S(1)}, s32[1,4]{1,0:T(1,128)}, u32[]{:S(2)}) copy-start(s32[1,4]{1,0:T(1,128)} %param.16) | copy-start | bytes 52
  19.0 69.4 %copy-start.4 = (bf16[9,32,128]{2,1,0:T(8,128)(2,1)S(1)}, bf16[9,32,128]{2,1,0:T(8,128)(2,1)}, u32[]{:S(2)}) copy-start(bf16[9,32,128]{2,1,0:T(8,128)(2,1)} %param.19) | copy-start | bytes 221188
  73.6 2.6 %collective-permute-start = (bf16[1,16,32]{2,1,0:T(8,128)(2,1)S(1)}, bf16[1,16,32]{2,1,0:T(8,128)(2,1)S(1)}, u32[]{:S(2)}, u32[]{:S(2)}) collective-permute-start(bf16[1,16,32]{2,1,0:T(8,128)(2,1)S(1)} %get-tuple-element.195), channel_id=1, source_target_pairs={{0,4},{4,8},{8,12},{1,5},{5,9},{9,13},{2,6},{6,10},{10,14},{3,7},{... | collective-permute-start | bytes 3080 | tf_op jit(solution)/shard_map/ppermute | solution.py:19
  74.9 4.4 %collective-permute-start.1 = (bf16[1,16,32]{2,1,0:T(8,128)(2,1)S(1)}, bf16[1,16,32]{2,1,0:T(8,128)(2,1)S(1)}, u32[]{:S(2)}, u32[]{:S(2)}) collective-permute-start(bf16[1,16,32]{2,1,0:T(8,128)(2,1)S(1)} %get-tuple-element.196), channel_id=1, source_target_pairs={{4,0},{8,4},{12,8},{5,1},{9,5},{13,9},{6,2},{10,6},{14,10},{7,3},{... | collective-permute-start | bytes 3080 | tf_op jit(solution)/shard_map/ppermute | solution.py:20
  79.3 9.2 %collective-permute-start.2 = (bf16[18,1,32]{2,1,0:T(2,128)(2,1)S(1)}, bf16[18,1,32]{2,1,0:T(2,128)(2,1)S(1)}, u32[]{:S(2)}, u32[]{:S(2)}) collective-permute-start(bf16[18,1,32]{2,1,0:T(2,128)(2,1)S(1)} %get-tuple-element.183), channel_id=1, source_target_pairs={{0,1},{1,2},{2,3},{4,5},{5,6},{6,7},{8,9},{9,10},{10,11},{12,13},{... | collective-permute-start | bytes 3464 | tf_op jit(solution)/shard_map/ppermute | solution.py:19
  86.4 5.0 %collective-permute-start.3 = (bf16[18,1,32]{2,1,0:T(2,128)(2,1)S(1)}, bf16[18,1,32]{2,1,0:T(2,128)(2,1)S(1)}, u32[]{:S(2)}, u32[]{:S(2)}) collective-permute-start(bf16[18,1,32]{2,1,0:T(2,128)(2,1)S(1)} %get-tuple-element.184), channel_id=1, source_target_pairs={{1,0},{2,1},{3,2},{5,4},{6,5},{7,6},{9,8},{10,9},{11,10},{13,12},{... | collective-permute-start | bytes 3464 | tf_op jit(solution)/shard_map/ppermute | solution.py:20
  88.4 17.4 %copy-start = (bf16[9,128,128]{2,1,0:T(8,128)(2,1)S(1)}, bf16[9,128,128]{2,1,0:T(8,128)(2,1)}, u32[]{:S(2)}) copy-start(bf16[9,128,128]{2,1,0:T(8,128)(2,1)} %param.20) | copy-start | bytes 884740
  92.7 4.7 %collective-permute-start.4 = (bf16[1,16,128]{2,1,0:T(8,128)(2,1)S(1)}, bf16[1,16,128]{2,1,0:T(8,128)(2,1)S(1)}, u32[]{:S(2)}, u32[]{:S(2)}) collective-permute-start(bf16[1,16,128]{2,1,0:T(8,128)(2,1)S(1)} %get-tuple-element.191), channel_id=1, source_target_pairs={{0,4},{4,8},{8,12},{1,5},{5,9},{9,13},{2,6},{6,10},{10,14},{3,7},{... | collective-permute-start | bytes 12296 | tf_op jit(solution)/shard_map/ppermute | solution.py:19
  96.1 4.4 %collective-permute-start.5 = (bf16[1,16,128]{2,1,0:T(8,128)(2,1)S(1)}, bf16[1,16,128]{2,1,0:T(8,128)(2,1)S(1)}, u32[]{:S(2)}, u32[]{:S(2)}) collective-permute-start(bf16[1,16,128]{2,1,0:T(8,128)(2,1)S(1)} %get-tuple-element.192), channel_id=1, source_target_pairs={{4,0},{8,4},{12,8},{5,1},{9,5},{13,9},{6,2},{10,6},{14,10},{7,3},{... | collective-permute-start | bytes 12296 | tf_op jit(solution)/shard_map/ppermute | solution.py:20
  100.4 5.5 %collective-permute-start.6 = (bf16[18,1,128]{2,1,0:T(2,128)(2,1)S(1)}, bf16[18,1,128]{2,1,0:T(2,128)(2,1)S(1)}, u32[]{:S(2)}, u32[]{:S(2)}) collective-permute-start(bf16[18,1,128]{2,1,0:T(2,128)(2,1)S(1)} %get-tuple-element.179), channel_id=1, source_target_pairs={{0,1},{1,2},{2,3},{4,5},{5,6},{6,7},{8,9},{9,10},{10,11},{12,13},{... | collective-permute-start | bytes 13832 | tf_op jit(solution)/shard_map/ppermute | solution.py:19
  103.8 5.0 %collective-permute-start.7 = (bf16[18,1,128]{2,1,0:T(2,128)(2,1)S(1)}, bf16[18,1,128]{2,1,0:T(2,128)(2,1)S(1)}, u32[]{:S(2)}, u32[]{:S(2)}) collective-permute-start(bf16[18,1,128]{2,1,0:T(2,128)(2,1)S(1)} %get-tuple-element.180), channel_id=1, source_target_pairs={{1,0},{2,1},{3,2},{5,4},{6,5},{7,6},{9,8},{10,9},{11,10},{13,12},{... | collective-permute-start | bytes 13832 | tf_op jit(solution)/shard_map/ppermute | solution.py:20
  105.9 16.1 %copy-start.1 = (bf16[9,128,128]{2,1,0:T(8,128)(2,1)S(1)}, bf16[9,128,128]{2,1,0:T(8,128)(2,1)}, u32[]{:S(2)}) copy-start(bf16[9,128,128]{2,1,0:T(8,128)(2,1)} %param.21) | copy-start | bytes 884740
  110.2 3.5 %collective-permute-start.8 = (bf16[1,16,128]{2,1,0:T(8,128)(2,1)S(1)}, bf16[1,16,128]{2,1,0:T(8,128)(2,1)S(1)}, u32[]{:S(2)}, u32[]{:S(2)}) collective-permute-start(bf16[1,16,128]{2,1,0:T(8,128)(2,1)S(1)} %get-tuple-element.187), channel_id=1, source_target_pairs={{0,4},{4,8},{8,12},{1,5},{5,9},{9,13},{2,6},{6,10},{10,14},{3,7},{... | collective-permute-start | bytes 12296 | tf_op jit(solution)/shard_map/ppermute | solution.py:19
  112.3 4.4 %collective-permute-start.9 = (bf16[1,16,128]{2,1,0:T(8,128)(2,1)S(1)}, bf16[1,16,128]{2,1,0:T(8,128)(2,1)S(1)}, u32[]{:S(2)}, u32[]{:S(2)}) collective-permute-start(bf16[1,16,128]{2,1,0:T(8,128)(2,1)S(1)} %get-tuple-element.188), channel_id=1, source_target_pairs={{4,0},{8,4},{12,8},{5,1},{9,5},{13,9},{6,2},{10,6},{14,10},{7,3},{... | collective-permute-start | bytes 12296 | tf_op jit(solution)/shard_map/ppermute | solution.py:20
  116.7 5.5 %collective-permute-start.10 = (bf16[18,1,128]{2,1,0:T(2,128)(2,1)S(1)}, bf16[18,1,128]{2,1,0:T(2,128)(2,1)S(1)}, u32[]{:S(2)}, u32[]{:S(2)}) collective-permute-start(bf16[18,1,128]{2,1,0:T(2,128)(2,1)S(1)} %get-tuple-element.175), channel_id=1, source_target_pairs={{0,1},{1,2},{2,3},{4,5},{5,6},{6,7},{8,9},{9,10},{10,11},{12,13},{... | collective-permute-start | bytes 13832 | tf_op jit(solution)/shard_map/ppermute | solution.py:19
  120.1 5.0 %collective-permute-start.11 = (bf16[18,1,128]{2,1,0:T(2,128)(2,1)S(1)}, bf16[18,1,128]{2,1,0:T(2,128)(2,1)S(1)}, u32[]{:S(2)}, u32[]{:S(2)}) collective-permute-start(bf16[18,1,128]{2,1,0:T(2,128)(2,1)S(1)} %get-tuple-element.176), channel_id=1, source_target_pairs={{1,0},{2,1},{3,2},{5,4},{6,5},{7,6},{9,8},{10,9},{11,10},{13,12},{... | collective-permute-start | bytes 13832 | tf_op jit(solution)/shard_map/ppermute | solution.py:20
Sparse Core Ops, SparseCore 0:
  52.1 20.6 reduce-scatter.1
where the time goes:
time: 135 us; the launch traced here: 134 us
  waiting for transfers between devices  38.6 us (29%)
  starting transfers between devices  30.3 us (22%)
  local copies, waits for them, and re-layouts  22.4 us (17%)
  between operations  13.9 us (10%)
  blocking collectives  11.3 us (8%)
  matrix products  9.79 us (7%)
  other arithmetic  7.22 us (5%)
    reduce_scatter x1, waiting for transfers between devices, shards(): lax.psum_scatter((colour * jnp.exp(-front)).astype(jnp.bfloat16), 'depth'...  20.8 us
    ppermute x6, starting transfers between devices, padded_2(): before = lax.ppermute(last, axis, up)  20.7 us
    ppermute x6, waiting for transfers between devices, padded_2(): after = lax.ppermute(first, axis, down)  17.7 us
    all_gather x1, blocking collectives, shards(): all_depth = lax.all_gather(depth_sum, 'depth', axis=0, tiled=True)  11.3 us
    ppermute x6, starting transfers between devices, padded_2(): after = lax.ppermute(first, axis, down)  9.64 us
    reshape x1, local copies, waits for them, and re-layouts, shards(): brick_features.reshape(feat_count, windows, SAMPLES).transpose(1, 2, 0)  5.43 us
    dot_general x27, matrix products, convolve_valid(): jnp.dot(window, weights[tap], preferred_element_type=jnp.float32)  4.52 us
    gather x2, local copies, waits for them, and re-layouts, march_block(): jnp.take(table, following, axis=0)  3.91 us
  transfers between devices with their start and end apart: 13, of which 7 were waited for; matrix products, arithmetic and copies ran while one was open for 0% of the time, Pallas kernels for 0%

commit v1 on v0

--- a/solution.py
+++ b/solution.py
@@ -7,6 +7,27 @@
 SAMPLES = 16
 ROWS_OWN = 16
 COLS_DEV = 16
+
+
+def gather_around(x, axis, dim):
+    size, index, span = (lax.axis_size(axis), lax.axis_index(axis), x.shape[dim])
+    right = [(i, (i + 1) % size) for i in range(size)]
+    left = [(i, (i - 1) % size) for i in range(size)]
+    out = jnp.zeros((*x.shape[:dim], size * span, *x.shape[dim + 1 :]), x.dtype)
+    out = lax.dynamic_update_slice_in_dim(out, x, index * span, axis=dim)
+    from_left = from_right = x
+    middle = size // 2
+    for step in range(1, middle + 1):
+        from_left = lax.ppermute(from_left, axis, right)
+        out = lax.dynamic_update_slice_in_dim(
+            out, from_left, (index - step) % size * span, axis=dim
+        )
+        if step < size - middle:
+            from_right = lax.ppermute(from_right, axis, left)
+            out = lax.dynamic_update_slice_in_dim(
+                out, from_right, (index + step) % size * span, axis=dim
+            )
+    return out
 
 
 def padded_2(x, sides, width):
@@ -109,7 +130,7 @@
     )
     colour = jnp.transpose(colour_blocks, (1, 0, 2)).reshape(colour_blocks.shape[1], total_rays)
     depth_sum = depth_blocks.reshape(1, total_rays)
-    all_depth = lax.all_gather(depth_sum, "depth", axis=0, tiled=True)
+    all_depth = gather_around(depth_sum, "depth", 0)
     my_rank = ranks[lax.axis_index("depth")]
     ahead = (ranks < my_rank).astype(jnp.float32)[None, :]
     front = jnp.dot(ahead, all_depth, precision=lax.Precision.HIGHEST)

time: 135 us -> 129 us (0.956)
  blocking collectives: 11.3 us -> 0 us
  starting transfers between devices: 30.3 us -> 37.1 us
  waiting for transfers between devices: 38.6 us -> 37.1 us
    all_gather x1 -> x0, blocking collectives: 11.3 us -> none  [shards(): all_depth = lax.all_gather(depth_sum, 'depth', axis=0, tiled=True)]
    ppermute x0 -> x3, waiting for transfers between devices: none -> 4.32 us  [the longest x2 4.32 us: gather_around(): from_left = lax.ppermute(from_left, axis, right)]
    ppermute x0 -> x3, starting transfers between devices: none -> 4.27 us  [the longest x2 2.19 us: gather_around(): from_left = lax.ppermute(from_left, axis, right)]
    reduce_scatter x1, waiting for transfers between devices: 20.8 us -> 17.4 us  [shards(): lax.psum_scatter((colour * jnp.exp(-front)).astype(jnp.bfloat16), 'depth'...]
    ppermute x6, waiting for transfers between devices: 17.7 us -> 14.9 us  [padded_2(): after = lax.ppermute(first, axis, down)]
    ppermute x6, starting transfers between devices: 20.7 us -> 23.2 us  [padded_2(): before = lax.ppermute(last, axis, up)]
  transfers between devices with their start and end apart: 13 -> 16, of which waited for: 7 -> 9; matrix products, arithmetic and copies ran while one was open for 0% -> 1% of each run, Pallas kernels for 0% -> 0%
where the time goes in v1:
time: 129 us; the launch traced here: 128 us
  starting transfers between devices  37.1 us (29%)
  waiting for transfers between devices  37.1 us (29%)
  local copies, waits for them, and re-layouts  22.7 us (18%)
  between operations  14 us (11%)
  matrix products  9.77 us (8%)
  other arithmetic  7.33 us (6%)
    ppermute x6, starting transfers between devices, padded_2(): before = lax.ppermute(last, axis, up)  23.2 us
    reduce_scatter x1, waiting for transfers between devices, shards(): lax.psum_scatter((colour * jnp.exp(-front)).astype(jnp.bfloat16), 'depth'...  17.4 us
    ppermute x6, waiting for transfers between devices, padded_2(): after = lax.ppermute(first, axis, down)  14.9 us
    ppermute x6, starting transfers between devices, padded_2(): after = lax.ppermute(first, axis, down)  9.64 us
    reshape x1, local copies, waits for them, and re-layouts, shards(): brick_features.reshape(feat_count, windows, SAMPLES).transpose(1, 2, 0)  5.43 us
    dot_general x27, matrix products, convolve_valid(): jnp.dot(window, weights[tap], preferred_element_type=jnp.float32)  4.51 us
    ppermute x2, waiting for transfers between devices, gather_around(): from_left = lax.ppermute(from_left, axis, right)  4.32 us
    gather x2, local copies, waits for them, and re-layouts, march_block(): jnp.take(table, window_ids, axis=0)  3.91 us
  transfers between devices with their start and end apart: 16, of which 9 were waited for; matrix products, arithmetic and copies ran while one was open for 1% of the time, Pallas kernels for 0%

profile of v1, /device:TPU:1, one launch (start us, length us, event | category | flops | bytes accessed | tf_op | source)
XLA Modules:
  0.0 128.4 jit_solution(14020715099765495303)
XLA Ops:
  9.8 5.4 %reshape.274 = bf16[16,1024,16]{2,1,0:T(8,128)(2,1)} reshape(bf16[16,1,1,16384]{3,0,2,1:T(8,128)(2,1)} %param.13) | data formatting | bytes 1048576 | tf_op jit(solution)/shard_map/reshape | solution.py:92
  15.2 3.7 %copy.13 = bf16[1024,16,16]{0,2,1:T(8,128)(2,1)S(1)} copy(bf16[1024,16,16]{1,0,2:T(8,128)(2,1)} %bitcast.219) | data formatting | bytes 1048576 | tf_op jit(solution)/shard_map/transpose | solution.py:93
  19.1 19.6 %while.14 = (s32[]{:T(128)}, f32[2,32,512]{2,1,0:T(8,128)S(1)}, f32[2,512]{1,0:T(2,128)S(1)}, s32[2,512]{1,0:T(2,128)S(1)}, s32[2,512]{1,0:T(2,128)S(1)}, /*inde...) while((s32[]{:T(128)}, f32[2,32,512]{2,1,0:T(8,128)S(1)}, ...), condition=%wide.region_3.5_spmd, body=%wide.region_0.4_spmd.sunk | while | flops 110472448 | bytes 23171440 | solution.py:128
  19.2 2.0 %gather_fusion.1 = bf16[512,256]{1,0:T(8,128)(2,1)S(1)} fusion(bf16[1024,256]{1,0:T(8,128)(2,1)S(1)} %get-tuple-element.290, s32[1024]{0:T(1024)S(1)} %pad_clamp_fusion.5), kind=kCustom, calls=%fused_computation.clone.clone.1 | custom fusion | bytes 526336 | tf_op jit(solution)/shard_map/while/body/eval_jaxpr/jit(_take)/gather | solution.py:109
  21.4 2.0 %gather_fusion = bf16[512,256]{1,0:T(8,128)(2,1)S(1)} fusion(bf16[1024,256]{1,0:T(8,128)(2,1)S(1)} %get-tuple-element.290, s32[1024]{0:T(1024)S(1)} %pad_clamp_fusion.4), kind=kCustom, calls=%fused_computation.1.clone.clone.1 | custom fusion | bytes 526336 | tf_op jit(solution)/shard_map/while/body/eval_jaxpr/jit(_take)/gather | solution.py:109
  29.0 2.0 %gather_fusion.1 = bf16[512,256]{1,0:T(8,128)(2,1)S(1)} fusion(bf16[1024,256]{1,0:T(8,128)(2,1)S(1)} %get-tuple-element.290, s32[1024]{0:T(1024)S(1)} %pad_clamp_fusion.5), kind=kCustom, calls=%fused_computation.clone.clone.1 | custom fusion | bytes 526336 | tf_op jit(solution)/shard_map/while/body/eval_jaxpr/jit(_take)/gather | solution.py:109
  31.1 2.0 %gather_fusion = bf16[512,256]{1,0:T(8,128)(2,1)S(1)} fusion(bf16[1024,256]{1,0:T(8,128)(2,1)S(1)} %get-tuple-element.290, s32[1024]{0:T(1024)S(1)} %pad_clamp_fusion.4), kind=kCustom, calls=%fused_computation.1.clone.clone.1 | custom fusion | bytes 526336 | tf_op jit(solution)/shard_map/while/body/eval_jaxpr/jit(_take)/gather | solution.py:109
  38.7 2.2 %collective-permute-start = (f32[1,1024]{1,0:T(1,128)S(1)}, f32[1,1024]{1,0:T(1,128)S(1)}, u32[]{:S(2)}, u32[]{:S(2)}) collective-permute-start(f32[1,1024]{1,0:T(1,128)S(1)} %bitcast.261), channel_id=1, source_target_pairs={{0,4},{4,8},{8,12},{12,0},{1,5},{5,9},{9,13},{13,1},{2,6},{6,10},{... | collective-permute-start | bytes 12296 | tf_op jit(solution)/shard_map/ppermute | solution.py:21
  40.9 2.1 %collective-permute-start.1 = (f32[1,1024]{1,0:T(1,128)S(1)}, f32[1,1024]{1,0:T(1,128)S(1)}, u32[]{:S(2)}, u32[]{:S(2)}) collective-permute-start(f32[1,1024]{1,0:T(1,128)S(1)} %bitcast.262), channel_id=1, source_target_pairs={{0,12},{4,0},{8,4},{12,8},{1,13},{5,1},{9,5},{13,9},{2,14},{6,2},{... | collective-permute-start | bytes 12296 | tf_op jit(solution)/shard_map/ppermute | solution.py:26
  44.8 3.4 %collective-permute-done.2 = f32[1,1024]{1,0:T(1,128)S(1)} collective-permute-done((f32[1,1024]{1,0:T(1,128)S(1)}, f32[1,1024]{1,0:T(1,128)S(1)}, u32[]{:S(2)}, u32[]{:S(2)}) %collective-permute-start.2) | collective-permute-done | bytes 4128 | tf_op jit(solution)/shard_map/ppermute | solution.py:21
  49.7 17.4 %reduce-scatter.2.cloned.1.call-done = bf16[32,256]{1,0:T(8,128)(2,1)} async-done(((bf16[32,1024]{1,0:T(8,128)(2,1)}), bf16[32,256]{1,0:T(8,128)(2,1)}) %reduce-scatter.2.cloned.1.call-update) | async-done | bytes 16400 | tf_op jit(solution)/shard_map/reduce_scatter | solution.py:137
  70.5 3.0 %collective-permute-done.4 = bf16[1,16,32]{2,1,0:T(8,128)(2,1)S(1)} collective-permute-done((bf16[1,16,32]{2,1,0:T(8,128)(2,1)S(1)}, bf16[1,16,32]{2,1,0:T(8,128)(2,1)S(1)}, u32[]{:S(2)}, u32[]{:S(2)}) %collective-permute-start.4) | collective-permute-done | bytes 1056 | tf_op jit(solution)/shard_map/ppermute | solution.py:41
  73.6 7.1 %collective-permute-start.5 = (bf16[18,1,32]{2,1,0:T(2,128)(2,1)S(1)}, bf16[18,1,32]{2,1,0:T(2,128)(2,1)S(1)}, u32[]{:S(2)}, u32[]{:S(2)}) collective-permute-start(bf16[18,1,32]{2,1,0:T(2,128)(2,1)S(1)} %get-tuple-element.175), channel_id=1, source_target_pairs={{0,1},{1,2},{2,3},{4,5},{5,6},{6,7},{8,9},{9,10},{10,11},{12,13},{... | collective-permute-start | bytes 3464 | tf_op jit(solution)/shard_map/ppermute | solution.py:40
  80.7 1.9 %collective-permute-start.6 = (bf16[18,1,32]{2,1,0:T(2,128)(2,1)S(1)}, bf16[18,1,32]{2,1,0:T(2,128)(2,1)S(1)}, u32[]{:S(2)}, u32[]{:S(2)}) collective-permute-start(bf16[18,1,32]{2,1,0:T(2,128)(2,1)S(1)} %get-tuple-element.176), channel_id=1, source_target_pairs={{1,0},{2,1},{3,2},{5,4},{6,5},{7,6},{9,8},{10,9},{11,10},{13,12},{... | collective-permute-start | bytes 3464 | tf_op jit(solution)/shard_map/ppermute | solution.py:41
  82.8 2.9 %collective-permute-done.6 = bf16[18,1,32]{2,1,0:T(2,128)(2,1)S(1)} collective-permute-done((bf16[18,1,32]{2,1,0:T(2,128)(2,1)S(1)}, bf16[18,1,32]{2,1,0:T(2,128)(2,1)S(1)}, u32[]{:S(2)}, u32[]{:S(2)}) %collective-permute-start.6) | collective-permute-done | bytes 1184 | tf_op jit(solution)/shard_map/ppermute | solution.py:41
  86.9 3.4 %collective-permute-start.7 = (bf16[1,16,128]{2,1,0:T(8,128)(2,1)S(1)}, bf16[1,16,128]{2,1,0:T(8,128)(2,1)S(1)}, u32[]{:S(2)}, u32[]{:S(2)}) collective-permute-start(bf16[1,16,128]{2,1,0:T(8,128)(2,1)S(1)} %get-tuple-element.183), channel_id=1, source_target_pairs={{0,4},{4,8},{8,12},{1,5},{5,9},{9,13},{2,6},{6,10},{10,14},{3,7},{... | collective-permute-start | bytes 12296 | tf_op jit(solution)/shard_map/ppermute | solution.py:40
  91.7 3.0 %collective-permute-done.8 = bf16[1,16,128]{2,1,0:T(8,128)(2,1)S(1)} collective-permute-done((bf16[1,16,128]{2,1,0:T(8,128)(2,1)S(1)}, bf16[1,16,128]{2,1,0:T(8,128)(2,1)S(1)}, u32[]{:S(2)}, u32[]{:S(2)}) %collective-permute-start.8) | collective-permute-done | bytes 4128 | tf_op jit(solution)/shard_map/ppermute | solution.py:41
  94.7 1.9 %collective-permute-start.10 = (bf16[18,1,128]{2,1,0:T(2,128)(2,1)S(1)}, bf16[18,1,128]{2,1,0:T(2,128)(2,1)S(1)}, u32[]{:S(2)}, u32[]{:S(2)}) collective-permute-start(bf16[18,1,128]{2,1,0:T(2,128)(2,1)S(1)} %get-tuple-element.172), channel_id=1, source_target_pairs={{1,0},{2,1},{3,2},{5,4},{6,5},{7,6},{9,8},{10,9},{11,10},{13,12},{... | collective-permute-start | bytes 13832 | tf_op jit(solution)/shard_map/ppermute | solution.py:41
  96.6 3.6 %collective-permute-start.9 = (bf16[18,1,128]{2,1,0:T(2,128)(2,1)S(1)}, bf16[18,1,128]{2,1,0:T(2,128)(2,1)S(1)}, u32[]{:S(2)}, u32[]{:S(2)}) collective-permute-start(bf16[18,1,128]{2,1,0:T(2,128)(2,1)S(1)} %get-tuple-element.171), channel_id=1, source_target_pairs={{0,1},{1,2},{2,3},{4,5},{5,6},{6,7},{8,9},{9,10},{10,11},{12,13},{... | collective-permute-start | bytes 13832 | tf_op jit(solution)/shard_map/ppermute | solution.py:40
  102.4 2.1 %collective-permute-start.11 = (bf16[1,16,128]{2,1,0:T(8,128)(2,1)S(1)}, bf16[1,16,128]{2,1,0:T(8,128)(2,1)S(1)}, u32[]{:S(2)}, u32[]{:S(2)}) collective-permute-start(bf16[1,16,128]{2,1,0:T(8,128)(2,1)S(1)} %get-tuple-element.179), channel_id=1, source_target_pairs={{0,4},{4,8},{8,12},{1,5},{5,9},{9,13},{2,6},{6,10},{10,14},{3,7},{... | collective-permute-start | bytes 12296 | tf_op jit(solution)/shard_map/ppermute | solution.py:40
  105.9 3.0 %collective-permute-done.12 = bf16[1,16,128]{2,1,0:T(8,128)(2,1)S(1)} collective-permute-done((bf16[1,16,128]{2,1,0:T(8,128)(2,1)S(1)}, bf16[1,16,128]{2,1,0:T(8,128)(2,1)S(1)}, u32[]{:S(2)}, u32[]{:S(2)}) %collective-permute-start.12) | collective-permute-done | bytes 4128 | tf_op jit(solution)/shard_map/ppermute | solution.py:41
  108.9 5.6 %collective-permute-start.13 = (bf16[18,1,128]{2,1,0:T(2,128)(2,1)S(1)}, bf16[18,1,128]{2,1,0:T(2,128)(2,1)S(1)}, u32[]{:S(2)}, u32[]{:S(2)}) collective-permute-start(bf16[18,1,128]{2,1,0:T(2,128)(2,1)S(1)} %get-tuple-element.167), channel_id=1, source_target_pairs={{0,1},{1,2},{2,3},{4,5},{5,6},{6,7},{8,9},{9,10},{10,11},{12,13},{... | collective-permute-start | bytes 13832 | tf_op jit(solution)/shard_map/ppermute | solution.py:40
  114.6 1.9 %collective-permute-start.14 = (bf16[18,1,128]{2,1,0:T(2,128)(2,1)S(1)}, bf16[18,1,128]{2,1,0:T(2,128)(2,1)S(1)}, u32[]{:S(2)}, u32[]{:S(2)}) collective-permute-start(bf16[18,1,128]{2,1,0:T(2,128)(2,1)S(1)} %get-tuple-element.168), channel_id=1, source_target_pairs={{1,0},{2,1},{3,2},{5,4},{6,5},{7,6},{9,8},{10,9},{11,10},{13,12},{... | collective-permute-start | bytes 13832 | tf_op jit(solution)/shard_map/ppermute | solution.py:41
  116.7 2.9 %collective-permute-done.14 = bf16[18,1,128]{2,1,0:T(2,128)(2,1)S(1)} collective-permute-done((bf16[18,1,128]{2,1,0:T(2,128)(2,1)S(1)}, bf16[18,1,128]{2,1,0:T(2,128)(2,1)S(1)}, u32[]{:S(2)}, u32[]{:S(2)}) %collective-permute-start.14) | collective-permute-done | bytes 4640 | tf_op jit(solution)/shard_map/ppermute | solution.py:41
  (150 shorter events, 29.6 us)
Async XLA Ops:
  6.5 60.5 %reduce-scatter.2.cloned.1.call-start = ((), (), s32[]{:S(2)}) async-start(), calls=%async_computation.1 | async-start | bytes 81920 | tf_op jit(solution)/shard_map/reduce_scatter | solution.py:137
  15.2 3.9 %copy-start.2 = (bf16[128,33]{0,1:T(8,128)(2,1)S(1)}, bf16[128,33]{0,1:T(8,128)(2,1)}, u32[]{:S(2)}) copy-start(bf16[128,33]{0,1:T(8,128)(2,1)} %param.18) | copy-start | bytes 25348
  15.2 3.9 %copy-start.3 = (bf16[16,128]{1,0:T(8,128)(2,1)S(1)}, bf16[16,128]{1,0:T(8,128)(2,1)}, u32[]{:S(2)}) copy-start(bf16[16,128]{1,0:T(8,128)(2,1)} %param.17) | copy-start | bytes 12292
  19.1 24.9 %copy-start.5 = (s32[1,4]{1,0:T(1,128)S(1)}, s32[1,4]{1,0:T(1,128)}, u32[]{:S(2)}) copy-start(s32[1,4]{1,0:T(1,128)} %param.16) | copy-start | bytes 52
  19.1 63.5 %copy-start.4 = (bf16[9,32,128]{2,1,0:T(8,128)(2,1)S(1)}, bf16[9,32,128]{2,1,0:T(8,128)(2,1)}, u32[]{:S(2)}) copy-start(bf16[9,32,128]{2,1,0:T(8,128)(2,1)} %param.19) | copy-start | bytes 221188
  38.7 5.2 %collective-permute-start = (f32[1,1024]{1,0:T(1,128)S(1)}, f32[1,1024]{1,0:T(1,128)S(1)}, u32[]{:S(2)}, u32[]{:S(2)}) collective-permute-start(f32[1,1024]{1,0:T(1,128)S(1)} %bitcast.261), channel_id=1, source_target_pairs={{0,4},{4,8},{8,12},{12,0},{1,5},{5,9},{9,13},{13,1},{2,6},{6,10},{... | collective-permute-start | bytes 12296 | tf_op jit(solution)/shard_map/ppermute | solution.py:21
  40.9 3.8 %collective-permute-start.1 = (f32[1,1024]{1,0:T(1,128)S(1)}, f32[1,1024]{1,0:T(1,128)S(1)}, u32[]{:S(2)}, u32[]{:S(2)}) collective-permute-start(f32[1,1024]{1,0:T(1,128)S(1)} %bitcast.262), channel_id=1, source_target_pairs={{0,12},{4,0},{8,4},{12,8},{1,13},{5,1},{9,5},{13,9},{2,14},{6,2},{... | collective-permute-start | bytes 12296 | tf_op jit(solution)/shard_map/ppermute | solution.py:26
  43.9 4.3 %collective-permute-start.2 = (f32[1,1024]{1,0:T(1,128)S(1)}, f32[1,1024]{1,0:T(1,128)S(1)}, u32[]{:S(2)}, u32[]{:S(2)}) collective-permute-start(f32[1,1024]{1,0:T(1,128)S(1)} %collective-permute-done), channel_id=1, source_target_pairs={{0,4},{4,8},{8,12},{12,0},{1,5},{5,9},{9,13},{13,1},{2,6},{6,10},{... | collective-permute-start | bytes 12296 | tf_op jit(solution)/shard_map/ppermute | solution.py:21
  67.9 2.6 %collective-permute-start.3 = (bf16[1,16,32]{2,1,0:T(8,128)(2,1)S(1)}, bf16[1,16,32]{2,1,0:T(8,128)(2,1)S(1)}, u32[]{:S(2)}, u32[]{:S(2)}) collective-permute-start(bf16[1,16,32]{2,1,0:T(8,128)(2,1)S(1)} %get-tuple-element.187), channel_id=1, source_target_pairs={{0,4},{4,8},{8,12},{1,5},{5,9},{9,13},{2,6},{6,10},{10,14},{3,7},{... | collective-permute-start | bytes 3080 | tf_op jit(solution)/shard_map/ppermute | solution.py:40
  69.2 4.4 %collective-permute-start.4 = (bf16[1,16,32]{2,1,0:T(8,128)(2,1)S(1)}, bf16[1,16,32]{2,1,0:T(8,128)(2,1)S(1)}, u32[]{:S(2)}, u32[]{:S(2)}) collective-permute-start(bf16[1,16,32]{2,1,0:T(8,128)(2,1)S(1)} %get-tuple-element.188), channel_id=1, source_target_pairs={{4,0},{8,4},{12,8},{5,1},{9,5},{13,9},{6,2},{10,6},{14,10},{7,3},{... | collective-permute-start | bytes 3080 | tf_op jit(solution)/shard_map/ppermute | solution.py:41
  73.6 9.2 %collective-permute-start.5 = (bf16[18,1,32]{2,1,0:T(2,128)(2,1)S(1)}, bf16[18,1,32]{2,1,0:T(2,128)(2,1)S(1)}, u32[]{:S(2)}, u32[]{:S(2)}) collective-permute-start(bf16[18,1,32]{2,1,0:T(2,128)(2,1)S(1)} %get-tuple-element.175), channel_id=1, source_target_pairs={{0,1},{1,2},{2,3},{4,5},{5,6},{6,7},{8,9},{9,10},{10,11},{12,13},{... | collective-permute-start | bytes 3464 | tf_op jit(solution)/shard_map/ppermute | solution.py:40
  80.7 5.0 %collective-permute-start.6 = (bf16[18,1,32]{2,1,0:T(2,128)(2,1)S(1)}, bf16[18,1,32]{2,1,0:T(2,128)(2,1)S(1)}, u32[]{:S(2)}, u32[]{:S(2)}) collective-permute-start(bf16[18,1,32]{2,1,0:T(2,128)(2,1)S(1)} %get-tuple-element.176), channel_id=1, source_target_pairs={{1,0},{2,1},{3,2},{5,4},{6,5},{7,6},{9,8},{10,9},{11,10},{13,12},{... | collective-permute-start | bytes 3464 | tf_op jit(solution)/shard_map/ppermute | solution.py:41
  82.7 17.7 %copy-start = (bf16[9,128,128]{2,1,0:T(8,128)(2,1)S(1)}, bf16[9,128,128]{2,1,0:T(8,128)(2,1)}, u32[]{:S(2)}) copy-start(bf16[9,128,128]{2,1,0:T(8,128)(2,1)} %param.20) | copy-start | bytes 884740
  86.9 4.7 %collective-permute-start.7 = (bf16[1,16,128]{2,1,0:T(8,128)(2,1)S(1)}, bf16[1,16,128]{2,1,0:T(8,128)(2,1)S(1)}, u32[]{:S(2)}, u32[]{:S(2)}) collective-permute-start(bf16[1,16,128]{2,1,0:T(8,128)(2,1)S(1)} %get-tuple-element.183), channel_id=1, source_target_pairs={{0,4},{4,8},{8,12},{1,5},{5,9},{9,13},{2,6},{6,10},{10,14},{3,7},{... | collective-permute-start | bytes 12296 | tf_op jit(solution)/shard_map/ppermute | solution.py:40
  90.3 4.4 %collective-permute-start.8 = (bf16[1,16,128]{2,1,0:T(8,128)(2,1)S(1)}, bf16[1,16,128]{2,1,0:T(8,128)(2,1)S(1)}, u32[]{:S(2)}, u32[]{:S(2)}) collective-permute-start(bf16[1,16,128]{2,1,0:T(8,128)(2,1)S(1)} %get-tuple-element.184), channel_id=1, source_target_pairs={{4,0},{8,4},{12,8},{5,1},{9,5},{13,9},{6,2},{10,6},{14,10},{7,3},{... | collective-permute-start | bytes 12296 | tf_op jit(solution)/shard_map/ppermute | solution.py:41
  94.7 5.8 %collective-permute-start.10 = (bf16[18,1,128]{2,1,0:T(2,128)(2,1)S(1)}, bf16[18,1,128]{2,1,0:T(2,128)(2,1)S(1)}, u32[]{:S(2)}, u32[]{:S(2)}) collective-permute-start(bf16[18,1,128]{2,1,0:T(2,128)(2,1)S(1)} %get-tuple-element.172), channel_id=1, source_target_pairs={{1,0},{2,1},{3,2},{5,4},{6,5},{7,6},{9,8},{10,9},{11,10},{13,12},{... | collective-permute-start | bytes 13832 | tf_op jit(solution)/shard_map/ppermute | solution.py:41
  96.6 4.4 %collective-permute-start.9 = (bf16[18,1,128]{2,1,0:T(2,128)(2,1)S(1)}, bf16[18,1,128]{2,1,0:T(2,128)(2,1)S(1)}, u32[]{:S(2)}, u32[]{:S(2)}) collective-permute-start(bf16[18,1,128]{2,1,0:T(2,128)(2,1)S(1)} %get-tuple-element.171), channel_id=1, source_target_pairs={{0,1},{1,2},{2,3},{4,5},{5,6},{6,7},{8,9},{9,10},{10,11},{12,13},{... | collective-permute-start | bytes 13832 | tf_op jit(solution)/shard_map/ppermute | solution.py:40
  100.5 16.0 %copy-start.1 = (bf16[9,128,128]{2,1,0:T(8,128)(2,1)S(1)}, bf16[9,128,128]{2,1,0:T(8,128)(2,1)}, u32[]{:S(2)}) copy-start(bf16[9,128,128]{2,1,0:T(8,128)(2,1)} %param.21) | copy-start | bytes 884740
  102.4 3.4 %collective-permute-start.11 = (bf16[1,16,128]{2,1,0:T(8,128)(2,1)S(1)}, bf16[1,16,128]{2,1,0:T(8,128)(2,1)S(1)}, u32[]{:S(2)}, u32[]{:S(2)}) collective-permute-start(bf16[1,16,128]{2,1,0:T(8,128)(2,1)S(1)} %get-tuple-element.179), channel_id=1, source_target_pairs={{0,4},{4,8},{8,12},{1,5},{5,9},{9,13},{2,6},{6,10},{10,14},{3,7},{... | collective-permute-start | bytes 12296 | tf_op jit(solution)/shard_map/ppermute | solution.py:40
  104.6 4.4 %collective-permute-start.12 = (bf16[1,16,128]{2,1,0:T(8,128)(2,1)S(1)}, bf16[1,16,128]{2,1,0:T(8,128)(2,1)S(1)}, u32[]{:S(2)}, u32[]{:S(2)}) collective-permute-start(bf16[1,16,128]{2,1,0:T(8,128)(2,1)S(1)} %get-tuple-element.180), channel_id=1, source_target_pairs={{4,0},{8,4},{12,8},{5,1},{9,5},{13,9},{6,2},{10,6},{14,10},{7,3},{... | collective-permute-start | bytes 12296 | tf_op jit(solution)/shard_map/ppermute | solution.py:41
  108.9 7.7 %collective-permute-start.13 = (bf16[18,1,128]{2,1,0:T(2,128)(2,1)S(1)}, bf16[18,1,128]{2,1,0:T(2,128)(2,1)S(1)}, u32[]{:S(2)}, u32[]{:S(2)}) collective-permute-start(bf16[18,1,128]{2,1,0:T(2,128)(2,1)S(1)} %get-tuple-element.167), channel_id=1, source_target_pairs={{0,1},{1,2},{2,3},{4,5},{5,6},{6,7},{8,9},{9,10},{10,11},{12,13},{... | collective-permute-start | bytes 13832 | tf_op jit(solution)/shard_map/ppermute | solution.py:40
  114.6 5.0 %collective-permute-start.14 = (bf16[18,1,128]{2,1,0:T(2,128)(2,1)S(1)}, bf16[18,1,128]{2,1,0:T(2,128)(2,1)S(1)}, u32[]{:S(2)}, u32[]{:S(2)}) collective-permute-start(bf16[18,1,128]{2,1,0:T(2,128)(2,1)S(1)} %get-tuple-element.168), channel_id=1, source_target_pairs={{1,0},{2,1},{3,2},{5,4},{6,5},{7,6},{9,8},{10,9},{11,10},{13,12},{... | collective-permute-start | bytes 13832 | tf_op jit(solution)/shard_map/ppermute | solution.py:41
Sparse Core Ops, SparseCore 0:
  49.8 17.1 reduce-scatter.1
